TPU v7x, 256 devices: a whole 4x4x8 slice. The times are simulated.
256 devices in a mesh: slide: 16 (over z, core), seg: 16 (over x, y).
Axes of the slice: x: 4, y: 4, z: 8, core: 2. Of those that a mesh axis runs over, the one named last changes fastest.
Arguments:
- tissue_counts: int32 [16], P('slide'), may hold values from 4096 to 8192, as said below
- block_moves: int32 [16, 16, 2, 4], P('slide', 'seg'), may hold values from 0 to 15, as said below
- queries: bfloat16 [16, 8192, 768], P('slide', 'seg'), may hold values from -6 to 6
- key_rows: bfloat16 [16, 8192, 768], P('slide', 'seg'), may hold values from -6 to 6
- values: bfloat16 [16, 8192, 768], P('slide', 'seg'), may hold values from -6 to 6
- forward_out: bfloat16 [16, 8192, 768], P('slide', 'seg'), may hold values from -3 to 3
- log_norms: float32 [16, 12, 8192], P('slide', None, 'seg'), may hold values from 7 to 9
- out_grads: bfloat16 [16, 8192, 768], P('slide', 'seg'), may hold values from -288 to 288
- proj_weights: bfloat16 [768, 2304], replicated, may hold values from -0.21875 to 0.21875
Outputs:
- packed_grads: bfloat16 [16, 8192, 768], P('slide', 'seg')
Inputs may be any that keep to these rules, and one draw needn't show every extreme that they name: Tissue tiles of each slide; the first tissue_counts[s] positions of slide s are tissue, the rest padding. One slide is full in every draw. Slot t of device (d, j) of the packed layout holds block block_moves[d, j, 1, t] of slide block_moves[d, j, 0, t] at the same seg index j, or is empty when that block index is 4. Each block that holds a position below its slide's tissue count sits in exactly one slot; no other block sits in any. One device of the packed layout holds at most 1 block of one slide, and some device holds 1 block of some slide.
All inputs are finite; a program needn't handle non-finite values.
Results may differ from a plain program's by a relative error of at most 0.0058.
Values may be sent and summed in bfloat16 or wider, within the bound.
A program may use at most 128 MiB of HBM per device.

v0:
```python
import jax
import jax.numpy as jnp
from jax import lax
from jax.experimental import pallas as pl
from jax.experimental.pallas import tpu as pltpu
from jax.sharding import PartitionSpec as P

D = 768
H = 12
R = 16
BLK = 128
ROWS = 512
HS = D // H
LANES = 128
PAIRS = D // LANES
N = 16
CHUNKS = 3
HALF = D // 2
BF = jnp.bfloat16
F32 = jnp.float32
MESH = pl.DeviceIdType.MESH


def dot(a, b):
    return jnp.dot(a, b, preferred_element_type=F32)


def dot_nt(a, b):
    return lax.dot_general(a, b, (((1,), (1,)), ((), ())), preferred_element_type=F32)


def await_bytes(ref, sem):
    pltpu.make_async_copy(ref, ref, sem).wait()


def transposed(x):
    return jnp.transpose(x.astype(F32)).astype(BF)


def row_dots(ones, grads, outs):
    product = grads.astype(F32) * outs.astype(F32)
    high = product.astype(BF)
    low = (product - high.astype(F32)).astype(BF)
    return dot_nt(ones, high) + dot_nt(ones, low)


def weigh(keys, query, norm):
    return jnp.exp(dot_nt(keys, query) - norm)


def attend(weights_of, keys_t, vals, query, grad, dots):
    value_parts, key_parts, query_t = [], [], None
    for i in range(2):
        rows = slice(256 * i, 256 * i + 256)
        weights = weights_of(rows)
        slopes = dot_nt(vals[rows], grad)
        scores = (weights * (slopes - dots)).astype(BF)
        value_parts.append(dot(weights.astype(BF), grad))
        key_parts.append(dot(scores, query))
        part = dot(keys_t[:, rows], scores)
        query_t = part if query_t is None else query_t + part
    return query_t, jnp.concatenate(key_parts, axis=0), jnp.concatenate(value_parts, axis=0)


def kernel(
    count_ref, moves_ref, q_hbm, k_hbm, v_hbm, o_hbm, norm_hbm, og_hbm, w_hbm, out_ref,
    qv, kv, vv, ov, nv, wv, k_t, tsend, trecv, tabv, tabs,
    ogv, ogf, ogd, sd, gdr, gmf,
    r1a, r1b, r1c, s2, gbuf, em, ebuf, nmsg, nbuf, gm, gdbuf, rsend, rbuf, held, tmp, acc, xs, total, mix,
    q1a, q1b, q1c, t2, in_sem, p1s, p1r, p1l, p2s, p2r, p2l, o1s, o1r, o1l, o2s, o2r, o2l,
    ss, rs, ls,
):
    me = lax.axis_index("slide")
    seg = lax.axis_index("seg")
    my_z, my_c = me // 2, me % 2
    r1, q1 = (r1a, r1b, r1c), (q1a, q1b, q1c)

    barrier = pltpu.get_barrier_semaphore()

    def greet(r, carry):
        pl.semaphore_signal(
            barrier, inc=1, device_id={"slide": lax.rem(me + r, N)}, device_id_type=MESH
        )
        pl.semaphore_signal(
            barrier, inc=1, device_id={"seg": lax.rem(seg + r, N)}, device_id_type=MESH
        )
        return carry

    lax.fori_loop(1, N, greet, 0)

    loads = [
        pltpu.make_async_copy(src, dst, in_sem.at[i])
        for i, (src, dst) in enumerate(
            (
                (og_hbm, ogv), (q_hbm, qv), (k_hbm, kv), (v_hbm, vv), (o_hbm, ov),
                (norm_hbm, nv),
            )
        )
    ]
    for k in range(CHUNKS):
        for n in range(3):
            for u in range(2):
                loads.append(
                    pltpu.make_async_copy(
                        w_hbm.at[:, pl.ds(n * D + u * HALF + k * LANES, LANES)],
                        wv.at[k, :, pl.ds((n * 2 + u) * LANES, LANES)],
                        in_sem.at[6],
                    )
                )
    for load in loads[:6]:
        load.start()

    lane = lax.broadcasted_iota(jnp.int32, (1, LANES), 1)
    table = jnp.zeros((1, LANES), jnp.int32)
    for t in range(4):
        block = moves_ref[1, t]
        code = jnp.where(block < 4, moves_ref[0, t] * 4 + block, 4 * N)
        table = jnp.where(lane == me * 4 + t, code, table)
    tsend[...] = table
    trecv[me] = table
    for buf in r1 + q1:
        buf[64:68] = jnp.zeros((4, 16, LANES), BF)
    gdr[N] = jnp.zeros((16, HALF), BF)

    pl.semaphore_wait(barrier, 2 * (N - 1))

    def far_first(r):
        step = (r // 2 + 1) // 2
        shift = jnp.where((r // 2) % 2 == 1, 4 - step, 4 + step)
        z = jnp.where(r == 14, my_z, lax.rem(my_z + shift, N // 2))
        return z * 2 + jnp.where(r == 14, 1 - my_c, lax.rem(my_c + r, 2))

    def columns(core, k):
        return pl.ds(pl.multiple_of(core * HALF + k * LANES, LANES), LANES)

    def send_table(r, carry):
        dest = lax.rem(me + r, N)
        pltpu.make_async_remote_copy(
            tsend, trecv.at[me], ss.at[0], rs.at[0], device_id={"slide": dest}, device_id_type=MESH
        ).start()
        return carry

    def spread(k, buf, source, send_sem, recv_sem, local_sem):
        slot = buf.at[pl.ds(me * 4, 4)]

        def one(r, carry):
            dest = far_first(r)
            pltpu.make_async_remote_copy(
                source(dest), slot, send_sem.at[k], recv_sem.at[k],
                device_id={"slide": dest}, device_id_type=MESH,
            ).start()
            return carry

        pltpu.make_async_copy(source(me), slot, local_sem.at[k]).start()
        lax.fori_loop(0, N - 1, one, 0)

    def deliver(k, buf, target, send_sem, recv_sem, local_sem):
        landing = target.at[:, my_z, :, columns(my_c, k)]

        def one(r, carry):
            dest = far_first(r)
            pltpu.make_async_remote_copy(
                buf.at[k, pl.ds(dest * 4, 4)], landing, send_sem.at[k], recv_sem.at[k],
                device_id={"slide": dest}, device_id_type=MESH,
            ).start()
            return carry

        pltpu.make_async_copy(buf.at[k, pl.ds(me * 4, 4)], landing, local_sem.at[k]).start()
        lax.fori_loop(0, N - 1, one, 0)

    def arrived(k, recv_sem, local_sem):
        await_bytes(s2.at[0, pl.ds(0, 60)], recv_sem.at[k])
        await_bytes(s2.at[0, pl.ds(0, 4)], local_sem.at[k])

    def choose(k, row, source, target):
        def one(i, carry):
            target[k, i] = source[tabs[row, i]]
            return carry

        lax.fori_loop(0, 4 * N, one, 0, unroll=8)

    lax.fori_loop(1, N, send_table, 0)
    def spread_in(k):
        spread(k, r1[k], lambda dest: og_hbm.at[:, dest // 2, :, columns(dest % 2, k)], p1s, p1r, p1l)

    spread_in(0)

    first = lax.broadcasted_iota(jnp.int32, (32, LANES), 1) < HS

    def dilate(ref, pair):
        return jnp.where(
            first,
            ref[pl.ds(2 * pair, 32, stride=R), :],
            ref[pl.ds(2 * pair + 1, 32, stride=R), :],
        )

    loads[0].wait()
    for pair in range(PAIRS):
        tmp[pair % 4] = ogv[:, :, :, pair * LANES : (pair + 1) * LANES].reshape(ROWS, LANES).astype(F32)
        picked = dilate(tmp.at[pair % 4], pair)
        up, cols = 8 * (pair // 3), slice((pair % 3) * LANES, (pair % 3 + 1) * LANES)
        for t in range(4):
            ogf[t, up : up + 8, cols] = picked[8 * t : 8 * t + 8]
    ogd[...] = ogf[...].astype(BF)

    def pick_slot(dest, carry):
        slot = jnp.int32(0)
        for t in range(4):
            slot = jnp.where((moves_ref[0, t] == dest) & (moves_ref[1, t] < 4), t, slot)
        sd[dest] = ogd[slot]
        return carry

    lax.fori_loop(0, N, pick_slot, 0)

    def send_dilated(r, carry):
        dest = far_first(r)
        pltpu.make_async_remote_copy(
            sd.at[dest], gdr.at[me], ss.at[5], rs.at[5], device_id={"slide": dest}, device_id_type=MESH
        ).start()
        return carry

    lax.fori_loop(0, N - 1, send_dilated, 0)
    pltpu.make_async_copy(sd.at[me], gdr.at[me], ls.at[5]).start()
    for k in range(1, CHUNKS):
        spread_in(k)
    for load in loads[6:]:
        load.start()

    for load in loads[1:6]:
        load.wait()
    alive = (lax.broadcasted_iota(jnp.int32, (ROWS, LANES), 0) + seg * ROWS) < count_ref[0]
    def prepare(pair, carry):
        cols = pl.ds(pl.multiple_of(pair * LANES, LANES), LANES)
        query = qv[:, cols].astype(F32) * (HS ** -0.5)
        keys = jnp.where(alive, kv[:, cols].astype(F32), 0.0)
        qv[:, cols] = query.astype(BF)
        kv[:, cols] = keys.astype(BF)
        k_t[pair] = jnp.transpose(keys).astype(BF)
        tmp[0] = query
        tmp[1] = keys
        tmp[2] = vv[:, cols].astype(F32)
        tmp[3] = ov[:, cols].astype(F32)
        for n in range(4):
            em[pair, n] = dilate(tmp.at[n], pair).astype(BF)
        return carry

    lax.fori_loop(0, PAIRS, prepare, 0)

    norms = nv[...].reshape(H, ROWS)
    head_row = lax.broadcasted_iota(jnp.int32, (H, ROWS), 0)
    head_lane = lax.broadcasted_iota(jnp.int32, (H, ROWS), 1)
    rest = jnp.where(head_lane % R == head_row, norms, 0.0)
    fold_row = lax.broadcasted_iota(jnp.int32, (ROWS, LANES), 0)
    fold_lane = lax.broadcasted_iota(jnp.int32, (ROWS, LANES), 1)
    fold = jnp.where(fold_row // R + 32 * (seg % 4) == fold_lane, 1.0, 0.0).astype(BF)
    folded = jnp.zeros((H, LANES), F32)
    for _ in range(3):
        piece = rest.astype(BF)
        folded = folded + dot(piece, fold)
        rest = rest - piece.astype(F32)
    for h in range(H):
        nmsg[h] = jnp.broadcast_to(folded[h : h + 1], (8, LANES))

    def send_head(src, dst, index, head):
        @pl.when(head != seg)
        def _():
            pltpu.make_async_remote_copy(
                src, dst, ss.at[index], rs.at[index], device_id={"seg": head}, device_id_type=MESH
            ).start()

        @pl.when(head == seg)
        def _():
            pltpu.make_async_copy(src, dst, ls.at[index]).start()

    def send_early(r, carry):
        head = lax.rem(seg + r, N)

        @pl.when(head < H)
        def _():
            send_head(em.at[head // 2], ebuf.at[seg], 1, head)
            send_head(nmsg.at[head], nbuf.at[seg], 2, head)

        return carry

    lax.fori_loop(0, N, send_early, 0)

    await_bytes(trecv.at[pl.ds(0, N - 1)], rs.at[0])
    codes = jnp.zeros((1, LANES), jnp.int32)
    for d in range(N):
        codes = codes + trecv[d]
    down = jnp.transpose(jnp.broadcast_to(codes.astype(F32), (LANES, LANES)))
    spot = lax.broadcasted_iota(jnp.int32, (LANES, LANES), 0)
    match = (down.astype(jnp.int32) == lax.broadcasted_iota(jnp.int32, (LANES, LANES), 1)) & (spot < 4 * N)
    inverse = jnp.sum(jnp.where(match, spot - 4 * N, 0), axis=0, keepdims=True) + 4 * N
    sub = lax.broadcasted_iota(jnp.int32, (8, LANES), 0)
    tabv[...] = jnp.clip(
        jnp.where(
            sub == 0, jnp.broadcast_to(inverse, (8, LANES)), jnp.broadcast_to(codes, (8, LANES))
        ),
        0,
        4 * N,
    )
    table_copy = pltpu.make_async_copy(tabv, tabs, ls.at[0])
    table_copy.start()
    table_copy.wait()

    def relay(k):
        arrived(k, p1r, p1l)
        choose(k, 0, r1[k], s2)
        deliver(k, s2, gbuf, p2s, p2r, p2l)

    relay(0)

    await_bytes(gdr.at[pl.ds(0, N - 1)], rs.at[5])
    await_bytes(gdr.at[0], ls.at[5])
    for b in range(4):
        got = gdr[tabs[0, me * 4 + b] // 4].astype(F32)
        for pair in range(PAIRS):
            up, cols = 8 * (pair // 3), slice((pair % 3) * LANES, (pair % 3 + 1) * LANES)
            gmf[pair, 8 * b : 8 * b + 8, :] = got[up : up + 8, cols]
    sparse_row = lax.broadcasted_iota(jnp.int32, (32, LANES), 0) * R + seg * ROWS
    for pair in range(PAIRS):
        position = sparse_row + jnp.where(first, 2 * pair, 2 * pair + 1)
        gm[pair] = jnp.where(position < count_ref[0], gmf[pair], 0.0).astype(BF)

    def send_grads(r, carry):
        head = lax.rem(seg + r, N)

        @pl.when(head < H)
        def _():
            send_head(gm.at[head // 2], gdbuf.at[seg], 3, head)

        return carry

    lax.fori_loop(0, N, send_grads, 0)

    wide_half = lax.broadcasted_iota(jnp.int32, (ROWS, LANES), 1) // HS

    def local_weights(k):
        def one(u, carry):
            pair = u * CHUNKS + k
            cols = pl.ds(pl.multiple_of(pair * LANES, LANES), LANES)
            query = qv[:, cols]
            for x in range(2):
                masked = jnp.where(wide_half == x, query, jnp.zeros((ROWS, LANES), BF))
                for i in range(2):
                    rows = slice(256 * i, 256 * i + 256)
                    held[2 * pair + x, rows, :] = weigh(kv[rows, cols], masked, nv[2 * pair + x])
            return carry

        lax.fori_loop(0, 2, one, 0)

    for k in range(1, CHUNKS):
        local_weights(k - 1)
        relay(k)

    ones_row = lax.broadcasted_iota(jnp.int32, (8, LANES), 0)
    ones_half = lax.broadcasted_iota(jnp.int32, (8, LANES), 1) // HS
    pair_ones = jnp.where(ones_row == ones_half, 1.0, 0.0).astype(BF)

    def sparse_head():
        await_bytes(ebuf.at[pl.ds(0, N - 1)], rs.at[1])
        await_bytes(ebuf.at[0], ls.at[1])
        await_bytes(nbuf.at[pl.ds(0, N - 1)], rs.at[2])
        await_bytes(nbuf.at[0], ls.at[2])
        await_bytes(gdbuf.at[pl.ds(0, N - 1)], rs.at[3])
        await_bytes(gdbuf.at[0], ls.at[3])
        mine = wide_half == seg % 2
        zero = jnp.zeros((ROWS, LANES), BF)
        query = jnp.where(mine, ebuf[:, 0].reshape(ROWS, LANES), zero)
        keys = jnp.where(mine, ebuf[:, 1].reshape(ROWS, LANES), zero)
        vals = ebuf[:, 2].reshape(ROWS, LANES)
        outs = ebuf[:, 3].reshape(ROWS, LANES)
        grad = jnp.where(mine, gdbuf[...].reshape(ROWS, LANES), zero)
        norm = jnp.concatenate(
            [
                sum(nbuf[4 * part + i, 0:1, :] for i in range(4))
                for part in range(4)
            ],
            axis=1,
        )
        dots = row_dots(jnp.ones((8, LANES), BF), grad, outs)[0:1]
        query_t, key_sum, value_sum = attend(
            lambda rows: weigh(keys[rows], query, norm), transposed(keys), vals, query, grad, dots
        )
        rsend[:, 0] = (jnp.transpose(query_t) * (HS ** -0.5)).astype(BF).reshape(N, 32, LANES)
        rsend[:, 1] = key_sum.astype(BF).reshape(N, 32, LANES)
        rsend[:, 2] = value_sum.astype(BF).reshape(N, 32, LANES)

        def back(r, carry):
            dest = lax.rem(seg + r, N)
            pltpu.make_async_remote_copy(
                rsend.at[dest], rbuf.at[seg], ss.at[4], rs.at[4],
                device_id={"seg": dest}, device_id_type=MESH,
            ).start()
            return carry

        lax.fori_loop(1, N, back, 0)
        pltpu.make_async_copy(rsend.at[seg], rbuf.at[seg], ls.at[4]).start()

    @pl.when(seg < H)
    def _():
        sparse_head()

    local_weights(CHUNKS - 1)

    def chunk(k, carry):
        arrived(k, p2r, p2l)

        def local_pair(u, inner):
            pair = u * CHUNKS + k
            cols = pl.ds(pl.multiple_of(pair * LANES, LANES), LANES)
            query, vals = qv[:, cols], vv[:, cols]
            grad = jnp.where(
                alive, gbuf[:, :, :, cols].reshape(ROWS, LANES).astype(F32), 0.0
            ).astype(BF)
            zero = jnp.zeros((ROWS, LANES), BF)
            dots = row_dots(pair_ones, grad, ov[:, cols])
            query_parts, key_sum, value_sum = [], None, None
            for x in range(2):
                mine = wide_half == x
                query_t, key_part, value_part = attend(
                    lambda rows, x=x: held[2 * pair + x, rows, :], k_t[pair, x * HS : (x + 1) * HS, :],
                    vals, jnp.where(mine, query, zero), jnp.where(mine, grad, zero), dots[x : x + 1],
                )
                query_parts.append(query_t)
                key_sum = key_part if key_sum is None else key_sum + key_part
                value_sum = value_part if value_sum is None else value_sum + value_part
            acc[0] = jnp.transpose(jnp.concatenate(query_parts, axis=0)) * (HS ** -0.5)
            acc[1] = key_sum
            acc[2] = value_sum

            @pl.when((u == 0) & (k == 0) & (seg < H))
            def _():
                await_bytes(rbuf.at[pl.ds(0, H - 1)], rs.at[4])
                await_bytes(rbuf.at[0], ls.at[4])

            @pl.when((u == 0) & (k == 0) & (seg >= H))
            def _():
                await_bytes(rbuf, rs.at[4])

            for n in range(3):
                place = acc.at[n]
                for x in range(2):
                    rows = pl.ds(2 * pair + x, 32, stride=R)
                    place[rows, :] = place[rows, :] + rbuf[2 * pair + x, n].astype(F32)
                where = pl.ds(pl.multiple_of((n * 2 + u) * LANES, LANES), LANES)
                xs[:, where] = place[...].astype(BF)
            return inner

        lax.fori_loop(0, 2, local_pair, 0)

        @pl.when(k == 0)
        def _():
            for load in loads[6:]:
                load.wait()
            total[...] = dot_nt(xs[...], wv[0])

        @pl.when(k == 1)
        def _():
            total[...] += dot_nt(xs[...], wv[1])

        return carry

    lax.fori_loop(0, CHUNKS, chunk, 0)

    for k in range(CHUNKS):
        for core in range(2):
            cols = slice(core * HALF + k * LANES, core * HALF + (k + 1) * LANES)
            mixed = total[:, cols] + dot_nt(xs[...], wv[CHUNKS - 1, cols, :])
            mix[k, core] = jnp.where(alive, mixed, 0.0).astype(BF).reshape(4, 8, 16, LANES)
        spread(
            k, q1[k], lambda dest, k=k: mix.at[k, dest % 2, :, dest // 2], o1s, o1r, o1l
        )

    for k in range(CHUNKS):
        arrived(k, o1r, o1l)
        choose(k, 4, q1[k], t2)
        deliver(k, t2, out_ref, o2s, o2r, o2l)
    for k in range(CHUNKS):
        arrived(k, o2r, o2l)

    for sems in (p1s, p2s, o1s, o2s):
        for k in range(CHUNKS):
            await_bytes(s2.at[0, pl.ds(0, 60)], sems.at[k])
    await_bytes(trecv.at[pl.ds(0, N - 1)], ss.at[0])
    await_bytes(gdr.at[pl.ds(0, N - 1)], ss.at[5])

    @pl.when(seg < H)
    def _():
        await_bytes(ebuf.at[pl.ds(0, H - 1)], ss.at[1])
        await_bytes(nbuf.at[pl.ds(0, H - 1)], ss.at[2])
        await_bytes(gdbuf.at[pl.ds(0, H - 1)], ss.at[3])
        await_bytes(rsend.at[pl.ds(0, N - 1)], ss.at[4])

    @pl.when(seg >= H)
    def _():
        await_bytes(ebuf.at[pl.ds(0, H)], ss.at[1])
        await_bytes(nbuf.at[pl.ds(0, H)], ss.at[2])
        await_bytes(gdbuf.at[pl.ds(0, H)], ss.at[3])


def shards(counts, moves, queries, key_rows, values, forward_out, log_norms, out_grads, weights):
    dma = pltpu.SemaphoreType.DMA
    vmem = pltpu.VMEM
    hbm_spec = pl.BlockSpec(memory_space=pltpu.HBM)
    smem_spec = pl.BlockSpec(memory_space=pltpu.SMEM)
    scratch = [
        *[vmem((ROWS, D), BF)] * 4,
        vmem((H, 1, ROWS), F32),
        vmem((CHUNKS, D, D), BF),
        vmem((PAIRS, LANES, ROWS), BF),
        vmem((1, LANES), jnp.int32),
        vmem((N, 1, LANES), jnp.int32),
        vmem((8, LANES), jnp.int32),
        pltpu.SMEM((8, LANES), jnp.int32),
        vmem((4, 8, 16, D), BF),
        vmem((4, 16, HALF), F32),
        vmem((4, 16, HALF), BF),
        vmem((N, 16, HALF), BF),
        vmem((N + 1, 16, HALF), BF),
        vmem((PAIRS, 32, LANES), F32),
        *[vmem((68, 16, LANES), BF)] * 3,
        vmem((CHUNKS, 64, 16, LANES), BF),
        vmem((4, 8, 16, D), BF),
        vmem((PAIRS, 4, 32, LANES), BF),
        vmem((N, 4, 32, LANES), BF),
        vmem((H, 8, LANES), F32),
        vmem((N, 8, LANES), F32),
        vmem((PAIRS, 32, LANES), BF),
        vmem((N, 32, LANES), BF),
        vmem((N, 3, 32, LANES), BF),
        vmem((H, 3, 32, LANES), BF),
        vmem((H, ROWS, ROWS), F32),
        vmem((4, ROWS, LANES), F32),
        vmem((3, ROWS, LANES), F32),
        vmem((ROWS, D), BF),
        vmem((ROWS, D), F32),
        vmem((CHUNKS, 2, 4, 8, 16, LANES), BF),
        *[vmem((68, 16, LANES), BF)] * 3,
        vmem((CHUNKS, 64, 16, LANES), BF),
        dma((7,)),
        *[dma((CHUNKS,))] * 12,
        *[dma((6,))] * 3,
    ]
    result = pl.pallas_call(
        kernel,
        out_shape=jax.ShapeDtypeStruct((4, 8, 16, D), BF),
        in_specs=[smem_spec, smem_spec] + [hbm_spec] * 7,
        out_specs=hbm_spec,
        scratch_shapes=scratch,
        compiler_params=pltpu.CompilerParams(
            collective_id=0, has_side_effects=True, vmem_limit_bytes=56 * 1024 * 1024
        ),
        name="dilated_backward",
    )(
        counts,
        moves[0, 0],
        queries[0],
        key_rows[0],
        values[0],
        forward_out[0],
        jnp.transpose(log_norms, (1, 0, 2)),
        out_grads[0].reshape(4, 8, 16, D),
        weights,
    )
    return result.reshape(1, ROWS, D)


def solution(mesh):
    return jax.shard_map(
        shards,
        mesh=mesh,
        in_specs=(
            P("slide"),
            P("slide", "seg", None, None),
            P("slide", "seg", None),
            P("slide", "seg", None),
            P("slide", "seg", None),
            P("slide", "seg", None),
            P("slide", None, "seg"),
            P("slide", "seg", None),
            P(),
        ),
        out_specs=P("slide", "seg", None),
        check_vma=False,
    )
```

profile of v0, /device:TPU:1, one launch (start us, length us, event | category | flops | bytes accessed | tf_op | source)
XLA Modules:
  0.0 94.8 jit_solution(8420615930949912781)
XLA Ops:
  0.7 92.1 %dilated_backward.1 = bf16[4,8,16,768]{3,2,1,0:T(8,128)(2,1)} custom-call(s32[1]{0:T(128)S(6)} %copy.11.count_ref, s32[2,4]{1,0:T(2,128)} %bitcast.15, bf16[512,768]{1,0:T(8,128)(2,1)} %bitcast.9, bf16[512,768]{1,0:T(8,128)(2,1)} %bitcast.10, bf16[512,768]{1,0:T(8,128)(2,1)} %bitcast.11, bf16[512,768]{1,0:T(8,128)(2,1)} %bitcast.12, f32[12,1,512]{2,1,0:T(1,128)} %bitcast.14, ...), custom_call_target="tpu_custom_call" | custom-call | tf_op jit(solution)/shard_map/dilated_backward/pallas_call | solution.py:546
  92.7 2.1 %copy.12 = bf16[1,512,768]{2,1,0:T(8,128)(2,1)} copy(bf16[1,512,768]{2,1,0:T(8,128)(2,1)} %bitcast.8) | data formatting | bytes 1572864
where the time goes:
time: 94.9 us; the launch traced here: 94.8 us
  Pallas kernels  92.1 us (97%)
  local copies, waits for them, and re-layouts  2.06 us (2%)
    pallas_call x1, Pallas kernels, shards(): pl.pallas_call(kernel, out_shape=jax.ShapeDtypeStruct((4, 8, 16, D), BF),...  92.1 us
    unnamed x1, local copies, waits for them, and re-layouts  2.06 us

commit v1 on v0

--- a/solution.py
+++ b/solution.py
@@ -16,6 +16,8 @@
 N = 16
 CHUNKS = 3
 HALF = D // 2
+AHEAD = (1, 2, 4, 5)
+AHEAD_COLS = 2 * LANES
 BF = jnp.bfloat16
 F32 = jnp.float32
 MESH = pl.DeviceIdType.MESH
@@ -120,7 +122,7 @@
     trecv[me] = table
     for buf in r1 + q1:
         buf[64:68] = jnp.zeros((4, 16, LANES), BF)
-    gdr[N] = jnp.zeros((16, HALF), BF)
+    gdr[N] = jnp.zeros((16, AHEAD_COLS), BF)
 
     pl.semaphore_wait(barrier, 2 * (N - 1))
 
@@ -195,10 +197,10 @@
         )
 
     loads[0].wait()
-    for pair in range(PAIRS):
+    for pair in AHEAD:
         tmp[pair % 4] = ogv[:, :, :, pair * LANES : (pair + 1) * LANES].reshape(ROWS, LANES).astype(F32)
         picked = dilate(tmp.at[pair % 4], pair)
-        up, cols = 8 * (pair // 3), slice((pair % 3) * LANES, (pair % 3 + 1) * LANES)
+        up, cols = 8 * (pair // 3), slice((pair % 3 - 1) * LANES, (pair % 3) * LANES)
         for t in range(4):
             ogf[t, up : up + 8, cols] = picked[8 * t : 8 * t + 8]
     ogd[...] = ogf[...].astype(BF)
@@ -309,31 +311,6 @@
         choose(k, 0, r1[k], s2)
         deliver(k, s2, gbuf, p2s, p2r, p2l)
 
-    relay(0)
-
-    await_bytes(gdr.at[pl.ds(0, N - 1)], rs.at[5])
-    await_bytes(gdr.at[0], ls.at[5])
-    for b in range(4):
-        got = gdr[tabs[0, me * 4 + b] // 4].astype(F32)
-        for pair in range(PAIRS):
-            up, cols = 8 * (pair // 3), slice((pair % 3) * LANES, (pair % 3 + 1) * LANES)
-            gmf[pair, 8 * b : 8 * b + 8, :] = got[up : up + 8, cols]
-    sparse_row = lax.broadcasted_iota(jnp.int32, (32, LANES), 0) * R + seg * ROWS
-    for pair in range(PAIRS):
-        position = sparse_row + jnp.where(first, 2 * pair, 2 * pair + 1)
-        gm[pair] = jnp.where(position < count_ref[0], gmf[pair], 0.0).astype(BF)
-
-    def send_grads(r, carry):
-        head = lax.rem(seg + r, N)
-
-        @pl.when(head < H)
-        def _():
-            send_head(gm.at[head // 2], gdbuf.at[seg], 3, head)
-
-        return carry
-
-    lax.fori_loop(0, N, send_grads, 0)
-
     wide_half = lax.broadcasted_iota(jnp.int32, (ROWS, LANES), 1) // HS
 
     def local_weights(k):
@@ -350,15 +327,41 @@
 
         lax.fori_loop(0, 2, one, 0)
 
+    local_weights(0)
+    local_weights(1)
+    relay(0)
+
+    await_bytes(gdr.at[pl.ds(0, N - 1)], rs.at[5])
+    await_bytes(gdr.at[0], ls.at[5])
+    for b in range(4):
+        got = gdr[tabs[0, me * 4 + b] // 4].astype(F32)
+        for pair in AHEAD:
+            up, cols = 8 * (pair // 3), slice((pair % 3 - 1) * LANES, (pair % 3) * LANES)
+            gmf[pair, 8 * b : 8 * b + 8, :] = got[up : up + 8, cols]
+    sparse_row = lax.broadcasted_iota(jnp.int32, (32, LANES), 0) * R + seg * ROWS
+    for pair in AHEAD:
+        position = sparse_row + jnp.where(first, 2 * pair, 2 * pair + 1)
+        gm[pair] = jnp.where(position < count_ref[0], gmf[pair], 0.0).astype(BF)
+
+    def send_grads(r, carry):
+        head = lax.rem(seg + r, N)
+
+        @pl.when((head < H) & ((head // 2) % CHUNKS != 0))
+        def _():
+            send_head(gm.at[head // 2], gdbuf.at[seg], 3, head)
+
+        return carry
+
+    lax.fori_loop(0, N, send_grads, 0)
+
     for k in range(1, CHUNKS):
-        local_weights(k - 1)
         relay(k)
 
     ones_row = lax.broadcasted_iota(jnp.int32, (8, LANES), 0)
     ones_half = lax.broadcasted_iota(jnp.int32, (8, LANES), 1) // HS
     pair_ones = jnp.where(ones_row == ones_half, 1.0, 0.0).astype(BF)
 
-    def sparse_head():
+    def sparse_head(index):
         await_bytes(ebuf.at[pl.ds(0, N - 1)], rs.at[1])
         await_bytes(ebuf.at[0], ls.at[1])
         await_bytes(nbuf.at[pl.ds(0, N - 1)], rs.at[2])
@@ -390,22 +393,55 @@
         def back(r, carry):
             dest = lax.rem(seg + r, N)
             pltpu.make_async_remote_copy(
-                rsend.at[dest], rbuf.at[seg], ss.at[4], rs.at[4],
+                rsend.at[dest], rbuf.at[seg], ss.at[index], rs.at[index],
                 device_id={"seg": dest}, device_id_type=MESH,
             ).start()
             return carry
 
         lax.fori_loop(1, N, back, 0)
-        pltpu.make_async_copy(rsend.at[seg], rbuf.at[seg], ls.at[4]).start()
-
-    @pl.when(seg < H)
+        pltpu.make_async_copy(rsend.at[seg], rbuf.at[seg], ls.at[index]).start()
+
+    owner_late = (seg < H) & ((seg // 2) % CHUNKS == 0)
+    owner_ahead = (seg < H) & ((seg // 2) % CHUNKS != 0)
+
+    @pl.when(owner_ahead)
     def _():
-        sparse_head()
+        sparse_head(4)
 
     local_weights(CHUNKS - 1)
+
+    def returned(index, count, mine):
+        @pl.when(mine)
+        def _():
+            await_bytes(rbuf.at[pl.ds(0, count - 1)], rs.at[index])
+            await_bytes(rbuf.at[0], ls.at[index])
+
+        @pl.when(jnp.logical_not(mine))
+        def _():
+            await_bytes(rbuf.at[pl.ds(0, count)], rs.at[index])
+
+    def merge(k, slot):
+        for u in range(2):
+            pair = u * CHUNKS + k
+            for n in range(3):
+                place = acc.at[k, u, n]
+                for x in range(2):
+                    rows = pl.ds(2 * pair + x, 32, stride=R)
+                    place[rows, :] = place[rows, :] + rbuf[2 * pair + x, n].astype(F32)
+                xs[slot, :, (n * 2 + u) * LANES : (n * 2 + u + 1) * LANES] = place[...].astype(BF)
 
     def chunk(k, carry):
         arrived(k, p2r, p2l)
+
+        @pl.when(k == 0)
+        def _():
+            for u in range(2):
+                pair = u * CHUNKS
+                cols = slice(pair * LANES, (pair + 1) * LANES)
+                tmp[u] = jnp.where(alive, gbuf[:, :, :, cols].reshape(ROWS, LANES).astype(F32), 0.0)
+                gm[pair] = dilate(tmp.at[u], pair).astype(BF)
+                send_head(gm.at[pair], gdbuf.at[seg], 3, 2 * pair)
+                send_head(gm.at[pair], gdbuf.at[seg], 3, 2 * pair + 1)
 
         def local_pair(u, inner):
             pair = u * CHUNKS + k
@@ -426,48 +462,36 @@
                 query_parts.append(query_t)
                 key_sum = key_part if key_sum is None else key_sum + key_part
                 value_sum = value_part if value_sum is None else value_sum + value_part
-            acc[0] = jnp.transpose(jnp.concatenate(query_parts, axis=0)) * (HS ** -0.5)
-            acc[1] = key_sum
-            acc[2] = value_sum
-
-            @pl.when((u == 0) & (k == 0) & (seg < H))
-            def _():
-                await_bytes(rbuf.at[pl.ds(0, H - 1)], rs.at[4])
-                await_bytes(rbuf.at[0], ls.at[4])
-
-            @pl.when((u == 0) & (k == 0) & (seg >= H))
-            def _():
-                await_bytes(rbuf, rs.at[4])
-
-            for n in range(3):
-                place = acc.at[n]
-                for x in range(2):
-                    rows = pl.ds(2 * pair + x, 32, stride=R)
-                    place[rows, :] = place[rows, :] + rbuf[2 * pair + x, n].astype(F32)
-                where = pl.ds(pl.multiple_of((n * 2 + u) * LANES, LANES), LANES)
-                xs[:, where] = place[...].astype(BF)
+            acc[k, u, 0] = jnp.transpose(jnp.concatenate(query_parts, axis=0)) * (HS ** -0.5)
+            acc[k, u, 1] = key_sum
+            acc[k, u, 2] = value_sum
             return inner
 
-        lax.fori_loop(0, 2, local_pair, 0)
-
-        @pl.when(k == 0)
+        lax.fori_loop(0, 2, local_pair, 0, unroll=True)
+
+        @pl.when((k == 0) & owner_late)
+        def _():
+            sparse_head(6)
+
+        @pl.when(k == 1)
         def _():
             for load in loads[6:]:
                 load.wait()
-            total[...] = dot_nt(xs[...], wv[0])
-
-        @pl.when(k == 1)
-        def _():
-            total[...] += dot_nt(xs[...], wv[1])
+            returned(4, 8, owner_ahead)
+            merge(1, 0)
+            total[...] = dot_nt(xs[0], wv[1])
 
         return carry
 
     lax.fori_loop(0, CHUNKS, chunk, 0)
+    returned(6, 4, owner_late)
+    merge(0, 0)
+    merge(CHUNKS - 1, 1)
 
     for k in range(CHUNKS):
         for core in range(2):
             cols = slice(core * HALF + k * LANES, core * HALF + (k + 1) * LANES)
-            mixed = total[:, cols] + dot_nt(xs[...], wv[CHUNKS - 1, cols, :])
+            mixed = total[:, cols] + dot_nt(xs[0], wv[0, cols, :]) + dot_nt(xs[1], wv[CHUNKS - 1, cols, :])
             mix[k, core] = jnp.where(alive, mixed, 0.0).astype(BF).reshape(4, 8, 16, LANES)
         spread(
             k, q1[k], lambda dest, k=k: mix.at[k, dest % 2, :, dest // 2], o1s, o1r, o1l
@@ -486,12 +510,19 @@
     await_bytes(trecv.at[pl.ds(0, N - 1)], ss.at[0])
     await_bytes(gdr.at[pl.ds(0, N - 1)], ss.at[5])
 
+    @pl.when(owner_ahead)
+    def _():
+        await_bytes(rsend.at[pl.ds(0, N - 1)], ss.at[4])
+
+    @pl.when(owner_late)
+    def _():
+        await_bytes(rsend.at[pl.ds(0, N - 1)], ss.at[6])
+
     @pl.when(seg < H)
     def _():
         await_bytes(ebuf.at[pl.ds(0, H - 1)], ss.at[1])
         await_bytes(nbuf.at[pl.ds(0, H - 1)], ss.at[2])
         await_bytes(gdbuf.at[pl.ds(0, H - 1)], ss.at[3])
-        await_bytes(rsend.at[pl.ds(0, N - 1)], ss.at[4])
 
     @pl.when(seg >= H)
     def _():
@@ -515,10 +546,10 @@
         vmem((8, LANES), jnp.int32),
         pltpu.SMEM((8, LANES), jnp.int32),
         vmem((4, 8, 16, D), BF),
-        vmem((4, 16, HALF), F32),
-        vmem((4, 16, HALF), BF),
-        vmem((N, 16, HALF), BF),
-        vmem((N + 1, 16, HALF), BF),
+        vmem((4, 16, AHEAD_COLS), F32),
+        vmem((4, 16, AHEAD_COLS), BF),
+        vmem((N, 16, AHEAD_COLS), BF),
+        vmem((N + 1, 16, AHEAD_COLS), BF),
         vmem((PAIRS, 32, LANES), F32),
         *[vmem((68, 16, LANES), BF)] * 3,
         vmem((CHUNKS, 64, 16, LANES), BF),
@@ -533,15 +564,15 @@
         vmem((H, 3, 32, LANES), BF),
         vmem((H, ROWS, ROWS), F32),
         vmem((4, ROWS, LANES), F32),
-        vmem((3, ROWS, LANES), F32),
-        vmem((ROWS, D), BF),
+        vmem((CHUNKS, 2, 3, ROWS, LANES), F32),
+        vmem((2, ROWS, D), BF),
         vmem((ROWS, D), F32),
         vmem((CHUNKS, 2, 4, 8, 16, LANES), BF),
         *[vmem((68, 16, LANES), BF)] * 3,
         vmem((CHUNKS, 64, 16, LANES), BF),
         dma((7,)),
         *[dma((CHUNKS,))] * 12,
-        *[dma((6,))] * 3,
+        *[dma((7,))] * 3,
     ]
     result = pl.pallas_call(
         kernel,

time: 94.9 us -> 93.6 us (0.986)
  Pallas kernels: 92.1 us -> 90.7 us
    pallas_call x1, Pallas kernels: 92.1 us -> 90.7 us  [shards(): pl.pallas_call(kernel, out_shape=jax.ShapeDtypeStruct((4, 8, 16, D), BF),...]
where the time goes in v1:
time: 93.6 us; the launch traced here: 93.5 us
  Pallas kernels  90.7 us (97%)
  local copies, waits for them, and re-layouts  2.06 us (2%)
    pallas_call x1, Pallas kernels, shards(): pl.pallas_call(kernel, out_shape=jax.ShapeDtypeStruct((4, 8, 16, D), BF),...  90.7 us
    unnamed x1, local copies, waits for them, and re-layouts  2.06 us

profile of v1, /device:TPU:1, one launch (start us, length us, event | category | flops | bytes accessed | tf_op | source)
XLA Modules:
  0.0 93.5 jit_solution(13410031730892078179)
XLA Ops:
  0.7 90.7 %dilated_backward.1 = bf16[4,8,16,768]{3,2,1,0:T(8,128)(2,1)} custom-call(s32[1]{0:T(128)S(6)} %copy.11.count_ref, s32[2,4]{1,0:T(2,128)} %bitcast.15, bf16[512,768]{1,0:T(8,128)(2,1)} %bitcast.9, bf16[512,768]{1,0:T(8,128)(2,1)} %bitcast.10, bf16[512,768]{1,0:T(8,128)(2,1)} %bitcast.11, bf16[512,768]{1,0:T(8,128)(2,1)} %bitcast.12, f32[12,1,512]{2,1,0:T(1,128)} %bitcast.14, ...), custom_call_target="tpu_custom_call" | custom-call | tf_op jit(solution)/shard_map/dilated_backward/pallas_call | solution.py:577
  91.4 2.1 %copy.12 = bf16[1,512,768]{2,1,0:T(8,128)(2,1)} copy(bf16[1,512,768]{2,1,0:T(8,128)(2,1)} %bitcast.8) | data formatting | bytes 1572864

commit v2 on v1

--- a/solution.py
+++ b/solution.py
@@ -198,7 +198,7 @@
 
     loads[0].wait()
     for pair in AHEAD:
-        tmp[pair % 4] = ogv[:, :, :, pair * LANES : (pair + 1) * LANES].reshape(ROWS, LANES).astype(F32)
+        tmp[pair % 4, :ROWS] = ogv[:, :, :, pair * LANES : (pair + 1) * LANES].reshape(ROWS, LANES).astype(F32)
         picked = dilate(tmp.at[pair % 4], pair)
         up, cols = 8 * (pair // 3), slice((pair % 3 - 1) * LANES, (pair % 3) * LANES)
         for t in range(4):
@@ -238,10 +238,10 @@
         qv[:, cols] = query.astype(BF)
         kv[:, cols] = keys.astype(BF)
         k_t[pair] = jnp.transpose(keys).astype(BF)
-        tmp[0] = query
-        tmp[1] = keys
-        tmp[2] = vv[:, cols].astype(F32)
-        tmp[3] = ov[:, cols].astype(F32)
+        tmp[0, :ROWS] = query
+        tmp[1, :ROWS] = keys
+        tmp[2, :ROWS] = vv[:, cols].astype(F32)
+        tmp[3, :ROWS] = ov[:, cols].astype(F32)
         for n in range(4):
             em[pair, n] = dilate(tmp.at[n], pair).astype(BF)
         return carry
@@ -428,7 +428,7 @@
                 for x in range(2):
                     rows = pl.ds(2 * pair + x, 32, stride=R)
                     place[rows, :] = place[rows, :] + rbuf[2 * pair + x, n].astype(F32)
-                xs[slot, :, (n * 2 + u) * LANES : (n * 2 + u + 1) * LANES] = place[...].astype(BF)
+                xs[slot, :, (n * 2 + u) * LANES : (n * 2 + u + 1) * LANES] = place[:ROWS, :].astype(BF)
 
     def chunk(k, carry):
         arrived(k, p2r, p2l)
@@ -438,7 +438,7 @@
             for u in range(2):
                 pair = u * CHUNKS
                 cols = slice(pair * LANES, (pair + 1) * LANES)
-                tmp[u] = jnp.where(alive, gbuf[:, :, :, cols].reshape(ROWS, LANES).astype(F32), 0.0)
+                tmp[u, :ROWS] = jnp.where(alive, gbuf[:, :, :, cols].reshape(ROWS, LANES).astype(F32), 0.0)
                 gm[pair] = dilate(tmp.at[u], pair).astype(BF)
                 send_head(gm.at[pair], gdbuf.at[seg], 3, 2 * pair)
                 send_head(gm.at[pair], gdbuf.at[seg], 3, 2 * pair + 1)
@@ -462,9 +462,9 @@
                 query_parts.append(query_t)
                 key_sum = key_part if key_sum is None else key_sum + key_part
                 value_sum = value_part if value_sum is None else value_sum + value_part
-            acc[k, u, 0] = jnp.transpose(jnp.concatenate(query_parts, axis=0)) * (HS ** -0.5)
-            acc[k, u, 1] = key_sum
-            acc[k, u, 2] = value_sum
+            acc[k, u, 0, :ROWS] = jnp.transpose(jnp.concatenate(query_parts, axis=0)) * (HS ** -0.5)
+            acc[k, u, 1, :ROWS] = key_sum
+            acc[k, u, 2, :ROWS] = value_sum
             return inner
 
         lax.fori_loop(0, 2, local_pair, 0, unroll=True)
@@ -563,8 +563,8 @@
         vmem((N, 3, 32, LANES), BF),
         vmem((H, 3, 32, LANES), BF),
         vmem((H, ROWS, ROWS), F32),
-        vmem((4, ROWS, LANES), F32),
-        vmem((CHUNKS, 2, 3, ROWS, LANES), F32),
+        vmem((4, ROWS + R, LANES), F32),
+        vmem((CHUNKS, 2, 3, ROWS + R, LANES), F32),
         vmem((2, ROWS, D), BF),
         vmem((ROWS, D), F32),
         vmem((CHUNKS, 2, 4, 8, 16, LANES), BF),

time: 93.6 us -> 93.6 us (level)
  no operation moved by 1% of the time
where the time goes in v2:
time: 93.6 us; the launch traced here: 93.5 us
  Pallas kernels  90.7 us (97%)
  local copies, waits for them, and re-layouts  2.06 us (2%)
    pallas_call x1, Pallas kernels, shards(): pl.pallas_call(kernel, out_shape=jax.ShapeDtypeStruct((4, 8, 16, D), BF),...  90.7 us
    unnamed x1, local copies, waits for them, and re-layouts  2.06 us

profile of v2, /device:TPU:1, one launch (start us, length us, event | category | flops | bytes accessed | tf_op | source)
XLA Modules:
  0.0 93.5 jit_solution(139134453776301175)
XLA Ops:
  0.7 90.7 %dilated_backward.1 = bf16[4,8,16,768]{3,2,1,0:T(8,128)(2,1)} custom-call(s32[1]{0:T(128)S(6)} %copy.11.count_ref, s32[2,4]{1,0:T(2,128)} %bitcast.15, bf16[512,768]{1,0:T(8,128)(2,1)} %bitcast.9, bf16[512,768]{1,0:T(8,128)(2,1)} %bitcast.10, bf16[512,768]{1,0:T(8,128)(2,1)} %bitcast.11, bf16[512,768]{1,0:T(8,128)(2,1)} %bitcast.12, f32[12,1,512]{2,1,0:T(1,128)} %bitcast.14, ...), custom_call_target="tpu_custom_call" | custom-call | tf_op jit(solution)/shard_map/dilated_backward/pallas_call | solution.py:577
  91.4 2.1 %copy.12 = bf16[1,512,768]{2,1,0:T(8,128)(2,1)} copy(bf16[1,512,768]{2,1,0:T(8,128)(2,1)} %bitcast.8) | data formatting | bytes 1572864
